TPU v7x, 32 devices: a whole 2x2x4 slice. The times are simulated.
32 devices in a mesh: groups: 2 (over y), seq: 4 (over z), tp: 2 (over x), section: 2 (over core).
Axes of the slice: x: 2, y: 2, z: 4, core: 2. Of those that a mesh axis runs over, the one named last changes fastest.
Arguments:
- page_pool: bfloat16 [384, 128, 576], P(('groups', 'seq', 'tp', 'section')), parts along dimension 0, as said below
- queries: bfloat16 [32, 64, 576], P(('groups', 'seq')), parts along dimension 0, as said below
- block_table: int32 [32, 2, 4], P(('groups', 'seq'), 'tp'), parts along dimension 0, may hold values from 0 to 11, as said below
- res_len: int32 [32, 2], P(('groups', 'seq'), 'tp'), parts along dimension 0, may hold values from 0 to 512, as said below
- piece_len: int32 [8, 2, 4], P(('groups', 'seq'), 'tp'), parts along dimension 0, may hold values from 1 to 512, 1024 in all within a row
- piece_owner: int32 [8, 2, 4], P(('groups', 'seq'), 'tp'), parts along dimension 0, may hold values from 0 to 3, each once within a row
- piece_slot: int32 [8, 2, 4], P(('groups', 'seq'), 'tp'), parts along dimension 0, may hold values from 0 to 3
- piece_pos: int32 [8, 2, 4], P(('groups', 'seq'), 'tp'), parts along dimension 0, may hold values from 0 to 8191
- kv_gain: float32 [512], replicated, may hold values from 0.25 to 1.75
Outputs:
- attended: bfloat16 [2, 32, 64, 512], P('section', ('groups', 'seq'), 'tp'), parts along dimension 1
There are 2 independent parts, one for each index of `groups`. A program takes and returns all parts, laid end to end along the dimension named above; an argument that names none is the same for every part. Nothing has to cross between parts.
Inputs may be any that keep to these rules, and one draw needn't show every extreme that they name: `block_table`: on each tp index of a row, the first ceil(res_len / 128) entries name distinct pages of that decode device, distinct from those of its other rows; the rest name pages too. `res_len`: every row has resident tokens on some tp index; on every decode device one row holds exactly 512 tokens. `piece_len`: the pieces of one prefill device sum to 1024 tokens; on every device one piece has exactly 512. `piece_owner`: each prefill device has exactly one piece for every decode owner. `page_pool`: entries lie within -20 and 20. `queries`: entries lie within -12 and 12.
All inputs are finite; a program needn't handle non-finite values.
Results may differ from a plain program's by a relative error of at most 0.0027.
Values may be sent and summed in bfloat16 or wider, within the bound.
A program may use at most 64 MiB of HBM per device.

v0:
```python
import jax
import jax.numpy as jnp
from jax import lax
from jax.sharding import PartitionSpec as P

FRESH_DEV = 1024


SOFT_SCALE = 192.0 ** (-0.5)
MASKED = -1e30
NORM_EPSILON = 1e-06


def passed_along(block, axis, distance):
    devices = range(lax.axis_size(axis))
    route = [(i - distance, i) for i in devices if i - distance in devices]
    return lax.ppermute(block, axis, route)


def combined_all(value, axis, join):
    pieces = jax.tree.map(lambda part: lax.all_gather(part, axis), value)
    head = jax.tree.map(lambda part: part[0], pieces)
    tail = jax.tree.map(lambda part: part[1:], pieces)
    so_far, _ = lax.scan(lambda so_far, piece: (join(so_far, piece), None), head, tail)
    return so_far


def rotate_half(rope_part, positions):
    half_width = rope_part.shape[-1] // 2
    inverse = 10000.0 ** (-jnp.arange(half_width, dtype=jnp.float32) / half_width)
    angles = positions.astype(jnp.float32)[:, None] * inverse[None, :]
    cosine = jnp.cos(angles)
    sine_part = jnp.sin(angles)
    first_half = rope_part[:, :half_width]
    second_half = rope_part[:, half_width:]
    return jnp.concatenate(
        [
            first_half * cosine - second_half * sine_part,
            second_half * cosine + first_half * sine_part,
        ],
        axis=1,
    )


def prepare_fresh(raw_tokens, kv_gain, piece_len, piece_pos):
    latent_width = kv_gain.shape[0]
    token_ids = jnp.arange(raw_tokens.shape[0], dtype=jnp.int32)
    piece_end = jnp.cumsum(piece_len)
    piece_begin = piece_end - piece_len
    owning = jnp.sum((token_ids[:, None] >= piece_end[None, :]).astype(jnp.int32), axis=1)
    selector = (owning[:, None] == jnp.arange(piece_len.shape[0], dtype=jnp.int32)[None, :]).astype(
        jnp.int32
    )
    positions = jnp.sum(selector * (piece_pos - piece_begin)[None, :], axis=1) + token_ids
    values = raw_tokens.astype(jnp.float32)
    latent = values[:, :latent_width]
    square_mean = jnp.mean(latent * latent, axis=1, keepdims=True)
    normed = latent * lax.rsqrt(square_mean + NORM_EPSILON) * kv_gain[None, :]
    rotated = rotate_half(values[:, latent_width:], positions)
    return jnp.concatenate([normed, rotated], axis=1).astype(jnp.bfloat16)


def pack_pieces(fresh, piece_len, piece_owner, piece_slot, capacity):
    peer_count = piece_len.shape[0]
    piece_begin = jnp.cumsum(piece_len) - piece_len
    matches = (piece_owner[None, :] == jnp.arange(peer_count, dtype=jnp.int32)[:, None]).astype(
        jnp.int32
    )
    send_len = jnp.sum(matches * piece_len[None, :], axis=1)
    send_begin = jnp.sum(matches * piece_begin[None, :], axis=1)
    send_slot = jnp.sum(matches * piece_slot[None, :], axis=1)
    columns = jnp.arange(capacity, dtype=jnp.int32)
    token_index = jnp.minimum(send_begin[:, None] + columns[None, :], fresh.shape[0] - 1)
    is_live = columns[None, :] < send_len[:, None]
    buffer = jnp.where(is_live[:, :, None], fresh[token_index], jnp.zeros((), jnp.bfloat16))
    return (buffer, jnp.stack([send_slot, send_len], axis=1))


def part_softmax(query_rows, key_rows, live_count, latent_width):
    scores = (
        jnp.einsum("bhc,bkc->bhk", query_rows, key_rows, preferred_element_type=jnp.float32)
        * SOFT_SCALE
    )
    is_live = (jnp.arange(key_rows.shape[1], dtype=jnp.int32)[None, :] < live_count[:, None])[
        :, None, :
    ]
    scores = jnp.where(is_live, scores, MASKED)
    row_max = jnp.max(scores, axis=2)
    weights = jnp.where(is_live, jnp.exp(scores - row_max[:, :, None]), 0.0)
    row_total = jnp.sum(weights, axis=2)
    row_out = jnp.einsum(
        "bhk,bkv->bhv",
        weights.astype(jnp.bfloat16),
        key_rows[:, :, :latent_width],
        preferred_element_type=jnp.float32,
    )
    return (row_max, row_total, row_out)


def owner_parts(query_rows, page_block, page_table, res_lens, handed, handed_meta, latent_width):
    row_count = query_rows.shape[0]
    gathered = page_block[page_table].reshape(row_count, -1, page_block.shape[2])
    res_max, res_total, res_out = part_softmax(query_rows, gathered, res_lens, latent_width)
    slot_ids = handed_meta[:, 0]
    piece_max, piece_total, piece_out = part_softmax(
        query_rows[slot_ids], handed, handed_meta[:, 1], latent_width
    )
    member = (slot_ids[None, :] == jnp.arange(row_count, dtype=jnp.int32)[:, None])[:, :, None]
    row_max = jnp.maximum(res_max, jnp.max(jnp.where(member, piece_max[None], MASKED), axis=1))
    res_weight = jnp.exp(res_max - row_max)
    piece_weight = jnp.exp(jnp.where(member, piece_max[None] - row_max[:, None], MASKED))
    row_total = res_total * res_weight + jnp.einsum(
        "rbh,bh->rh", piece_weight, piece_total, precision=lax.Precision.HIGHEST
    )
    row_out = res_out * res_weight[:, :, None] + jnp.einsum(
        "rbh,bhv->rhv", piece_weight, piece_out, precision=lax.Precision.HIGHEST
    )
    return (row_max, row_total, row_out)


def merge_parts(first, second):
    first_max, first_total, first_out = first
    second_max, second_total, second_out = second
    joint = jnp.maximum(first_max, second_max)
    first_weight = jnp.exp(first_max - joint)
    second_weight = jnp.exp(second_max - joint)
    return (
        joint,
        first_total * first_weight + second_total * second_weight,
        first_out * first_weight[:, :, None] + second_out * second_weight[:, :, None],
    )


def local(
    page_pool, queries, block_table, res_len, piece_len, piece_owner, piece_slot, piece_pos, kv_gain
):
    pages_here, page_width, full_width = page_pool.shape
    latent_width = kv_gain.shape[0]
    capacity = 2 * FRESH_DEV // lax.axis_size("seq")
    raw_tokens = page_pool.reshape(pages_here * page_width, full_width)[:FRESH_DEV]
    lengths = piece_len[0, 0]
    owners = piece_owner[0, 0]
    slot_list = piece_slot[0, 0]
    fresh = prepare_fresh(raw_tokens, kv_gain, lengths, piece_pos[0, 0])
    packed, packed_meta = pack_pieces(fresh, lengths, owners, slot_list, capacity)
    packed, packed_meta = (
        lax.all_to_all(packed, "seq", split_axis=0, concat_axis=0, tiled=True),
        lax.all_to_all(packed_meta, "seq", split_axis=0, concat_axis=0, tiled=True),
    )
    handed, handed_meta = passed_along((packed, packed_meta), "section", 1)
    is_decode = lax.axis_index("section") == 1
    row_count = queries.shape[0]
    head_count = queries.shape[1]

    def attend(unused):
        return owner_parts(
            queries, page_pool, block_table[:, 0], res_len[:, 0], handed, handed_meta, latent_width
        )

    def no_rows(unused):
        return (
            jnp.zeros((row_count, head_count), jnp.float32),
            jnp.ones((row_count, head_count), jnp.float32),
            jnp.zeros((row_count, head_count, latent_width), jnp.float32),
        )

    row_max, row_total, row_out = lax.cond(is_decode, attend, no_rows, 0)
    head_share = head_count // lax.axis_size("tp")
    row_max, row_total, row_out = combined_all((row_max, row_total, row_out), "tp", merge_parts)
    head_start = lax.axis_index("tp") * head_share
    row_total = lax.dynamic_slice_in_dim(row_total, head_start, head_share, 1)
    row_out = lax.dynamic_slice_in_dim(row_out, head_start, head_share, 1)
    result = jnp.where(is_decode, row_out / row_total[:, :, None], 0.0).astype(jnp.bfloat16)
    return result[None]


def solution(mesh):
    return jax.shard_map(
        local,
        mesh=mesh,
        in_specs=(
            P(("groups", "seq", "tp", "section"), None, None),
            P(("groups", "seq"), None, None),
            P(("groups", "seq"), "tp", None),
            P(("groups", "seq"), "tp"),
            P(("groups", "seq"), "tp", None),
            P(("groups", "seq"), "tp", None),
            P(("groups", "seq"), "tp", None),
            P(("groups", "seq"), "tp", None),
            P(),
        ),
        out_specs=P("section", ("groups", "seq"), "tp", None),
        check_vma=False,
    )
```

profile of v0, /device:TPU:1, one launch (start us, length us, event | category | flops | bytes accessed | tf_op | source)
XLA Modules:
  0.0 151.9 jit_solution(10688625318044384241)
XLA Ops:
  6.5 0.8 reduce-window.7
  7.4 0.7 bitcast_subtract_fusion
  8.1 0.8 select_reduce_fusion.2
  9.2 1.6 %copy_bitcast_fusion = f32[1024,576]{0,1:T(8,128)S(1)} fusion(bf16[12,128,576]{1,2,0:T(8,128)(2,1)} %param.11), kind=kLoop, calls=%fused_computation.50 | loop fusion | flops 589824 | bytes 3538944 | tf_op jit(solution)/shard_map/convert_element_type | solution.py:55
  11.9 0.7 copy.81
  12.6 9.3 %gather_fusion.2 = bf16[2048,576]{1,0:T(8,128)(2,1)} fusion(bf16[1024,576]{1,0:T(8,128)(2,1)S(1)} %copy.81, s32[2048]{0:T(1024)S(1)} %broadcast_clamp_fusion), kind=kCustom, calls=%fused_computation.2 | custom fusion | bytes 4726784 | tf_op jit(solution)/shard_map/gather | solution.py:75
  22.0 2.9 %copy.82 = bf16[4,512,576]{1,2,0:T(8,128)(2,1)S(1)} copy(bf16[4,512,576]{2,1,0:T(8,128)(2,1)} %bitcast.85) | data formatting | bytes 4718592 | tf_op jit(solution)/shard_map/gather | solution.py:75
  25.1 58.4 %all_to_all.17 = bf16[4,512,576]{1,2,0:T(8,128)(2,1)} all-to-all(bf16[4,512,576]{1,2,0:T(8,128)(2,1)S(1)} %broadcast_select_fusion), channel_id=1, replica_groups=mesh['groups'=2,'seq'=4,'tp'=2,'section'=2] {'seq'}, dimensions={0} | all-to-all | bytes 4718592 | tf_op jit(solution)/shard_map/all_to_all | solution.py:147
  83.5 1.3 collective-permute-start.1
  84.8 0.7 copy.78
  85.5 3.2 %all-to-all-start = ((s32[4,1,2]{2,1,0:T(1,128)}), s32[4,1,2]{2,1,0:T(1,128)S(1)}, u32[]{:S(2)}, u32[]{:S(2)}) async-start(s32[4,1,2]{2,1,0:T(1,128)} %copy.78), calls=%async_computation | async-start | bytes 4096 | tf_op jit(solution)/shard_map/all_to_all | solution.py:148
  88.8 4.3 %all-to-all-done = s32[4,1,2]{2,1,0:T(1,128)S(1)} async-done(((s32[4,1,2]{2,1,0:T(1,128)}), s32[4,1,2]{2,1,0:T(1,128)S(1)}, u32[]{:S(2)}, u32[]{:S(2)}) %all-to-all-start) | async-done | bytes 64 | tf_op jit(solution)/shard_map/all_to_all | solution.py:148
  93.1 1.3 collective-permute-start
  94.4 3.7 %collective-permute-done = s32[4,2]{0,1:T(2,128)S(1)} collective-permute-done((s32[4,2]{0,1:T(2,128)S(1)}, s32[4,2]{0,1:T(2,128)S(1)}, u32[]{:S(2)}, u32[]{:S(2)}) %collective-permute-start) | collective-permute-done | bytes 64 | tf_op jit(solution)/shard_map/ppermute | solution.py:17
  98.1 25.7 %conditional.1 = (f32[4,64]{1,0:T(4,128)}, f32[4,64]{1,0:T(4,128)}, f32[4,64,512]{2,1,0:T(8,128)}) conditional(s32[]{:T(128)} %convert_element_type.31, () %tuple.15, (s32[4,1]{0,1:T(1,128)S(1)}, s32[4,1,4]{2,1,0:T(1,128)S(1)}, bf16[12,128,576]{1,2,0:T(8,128)(2,1)}, bf16[4,64,576]{2,1,0:T(8,128)(2,1)S(1)}, s32[4,2]{0,1:T(2,128)S(1)}, ...), branch_computations={%region_7.8_spmd, %region_8.14_spmd} | conditional | flops 579352128 | bytes 35982092 | solution.py:167
  100.5 0.7 copy.93
  101.3 0.8 select_reduce_fusion
  102.8 2.6 %copy.85 = bf16[4,512,576]{2,1,0:T(8,128)(2,1)} copy(bf16[4,512,576]{1,2,0:T(8,128)(2,1)S(1)} %get-tuple-element.91) | data formatting | bytes 4718592 | tf_op jit(solution)/shard_map
  105.4 3.1 %fusion = f32[4,64,512]{2,1,0:T(8,128)} fusion(bf16[4,512,576]{2,1,0:T(8,128)(2,1)} %copy.85, f32[4,64,512]{2,1,0:T(8,128)S(1)} %get-tuple-element.108, f32[4,64]{1,0:T(4,128)S(1)} %get-tuple-element.107, pred[4,512]{1,0:T(4,128)(4,1)S(1)} %iota_compare_fusion), kind=kOutput, calls=%fused_computation.3 | convolution fusion | flops 134610944 | bytes 3148800 | tf_op jit(solution)/shard_map/cond/branch_1_fun/bhk,bkv->bhv/dot_general | solution.py:91
  108.4 2.3 %copy.84 = bf16[12,128,576]{2,1,0:T(8,128)(2,1)} copy(bf16[12,128,576]{1,2,0:T(8,128)(2,1)S(1)} %copy-done) | data formatting | bytes 3538944 | tf_op jit(solution)/shard_map
  110.7 2.6 %gather_fusion = bf16[16,128,576]{2,1,0:T(8,128)(2,1)S(1)} fusion(bf16[12,128,576]{2,1,0:T(8,128)(2,1)} %copy.84, s32[1024]{0:T(1024)S(1)} %pad_clamp_fusion.1), kind=kCustom, calls=%fused_computation | custom fusion | bytes 4718656 | tf_op jit(solution)/shard_map/cond/branch_1_fun/gather | solution.py:102
  113.3 1.0 fusion.56
  115.1 0.8 copy.75
  115.9 3.2 %fusion.13 = f32[64,512,4]{1,2,0:T(4,128)} fusion(f32[4,64,512]{2,1,0:T(8,128)} %fusion, f32[4,64]{0,1:T(8,128)S(1)} %copy.75, f32[4,64]{0,1:T(8,128)S(1)} %copy.73, pred[4,4]{1,0:T(4,128)(4,1)S(1)} %copy-done.3), kind=kOutput, calls=%fused_computation.14 | convolution fusion | flops 6293504 | bytes 1050640 | tf_op jit(solution)/shard_map/cond/branch_1_fun/rbh,bhv->rhv/dot_general | solution.py:115
  119.1 1.0 multiply_reduce_fusion
  120.1 1.3 bitcast_add_fusion
  121.4 2.4 %fusion.9 = f32[4,64,512]{2,1,0:T(8,128)} fusion(bf16[4,512,576]{2,1,0:T(8,128)(2,1)S(1)} %bitcast.84, f32[64,512,4]{1,2,0:T(4,128)} %fusion.13, f32[4,64,512]{2,1,0:T(8,128)S(1)} %get-tuple-element.106, f32[4,64]{1,0:T(4,128)S(1)} %get-tuple-element.96, f32[4,64]{1,0:T(4,128)S(1)} %get-tuple-element.105, pred[4,512]{1,0:T(4,128)(4,1)S(1)} %iota_compare_fusion.1), kind=kOutput, calls=%fused_computation.11 | convolution fusion | flops 134873088 | bytes 3676160 | tf_op jit(solution)/shard_map/cond/branch_1_fun/bhk,bkv->bhv/dot_general | solution.py:91
  123.9 3.4 %all-gather.3 = f32[2,4,64]{2,1,0:T(4,128)S(1)} all-gather(f32[1,4,64]{2,1,0:T(4,128)} %bitcast.23), channel_id=3, replica_groups=mesh['groups'=2,'seq'=4,'tp'=2,'section'=2] {'tp'}, dimensions={0}, use_global_device_ids=true | all-gather | bytes 3072 | tf_op jit(solution)/shard_map/all_gather | solution.py:21
  127.3 3.3 %all-gather.4 = f32[2,4,64]{2,1,0:T(4,128)S(1)} all-gather(f32[1,4,64]{2,1,0:T(4,128)} %bitcast.26), channel_id=4, replica_groups=mesh['groups'=2,'seq'=4,'tp'=2,'section'=2] {'tp'}, dimensions={0}, use_global_device_ids=true | all-gather | bytes 3072 | tf_op jit(solution)/shard_map/all_gather | solution.py:21
  130.7 12.3 %all-gather.7.cloned.1.call-done = f32[8,64,512]{2,1,0:T(8,128)} async-done(((f32[4,64,512]{2,1,0:T(8,128)}), f32[8,64,512]{2,1,0:T(8,128)}) %all-gather.7.cloned.1.call-update) | async-done | bytes 1048592 | tf_op jit(solution)/shard_map/all_gather | solution.py:21
  143.0 1.3 fusion.58
  144.3 0.8 fusion.47
  (52 shorter events, 5.9 us)
Async XLA Ops:
  9.2 2.4 %copy-start.5 = (f32[512]{0:T(512)S(1)}, f32[512]{0:T(512)}, u32[]{:S(2)}) copy-start(f32[512]{0:T(512)} %param.19) | copy-start | bytes 6148
  25.1 73.0 %copy-start.1 = (bf16[4,64,576]{2,1,0:T(8,128)(2,1)S(1)}, bf16[4,64,576]{2,1,0:T(8,128)(2,1)}, u32[]{:S(2)}) copy-start(bf16[4,64,576]{2,1,0:T(8,128)(2,1)} %param.12) | copy-start | bytes 884740
  25.1 73.0 %copy-start.4 = (s32[4,1,4]{2,1,0:T(1,128)S(1)}, s32[4,1,4]{2,1,0:T(1,128)}, u32[]{:S(2)}) copy-start(s32[4,1,4]{2,1,0:T(1,128)} %param.13) | copy-start | bytes 196
  25.1 73.0 %copy-start.6 = (s32[4,1]{0,1:T(1,128)S(1)}, s32[4,1]{0,1:T(1,128)}, u32[]{:S(2)}) copy-start(s32[4,1]{0,1:T(1,128)} %param.14) | copy-start | bytes 52
  83.5 14.6 %collective-permute-start.1 = (bf16[4,512,576]{1,2,0:T(8,128)(2,1)}, bf16[4,512,576]{1,2,0:T(8,128)(2,1)S(1)}, u32[]{:S(2)}, u32[]{:S(2)}) collective-permute-start(bf16[4,512,576]{1,2,0:T(8,128)(2,1)} %all_to_all.17), channel_id=1, source_target_pairs={{0,1},{2,3},{4,5},{6,7},{8,9},{10,11},{12,13},{14,15},{16,17},{18,... | collective-permute-start | bytes 7077896 | tf_op jit(solution)/shard_map/ppermute | solution.py:17
  85.5 7.5 %all-to-all-start = ((s32[4,1,2]{2,1,0:T(1,128)}), s32[4,1,2]{2,1,0:T(1,128)S(1)}, u32[]{:S(2)}, u32[]{:S(2)}) async-start(s32[4,1,2]{2,1,0:T(1,128)} %copy.78), calls=%async_computation | async-start | bytes 4096 | tf_op jit(solution)/shard_map/all_to_all | solution.py:148
  88.7 54.3 %all-gather.7.cloned.1.call-start = ((), (), s32[]{:S(2)}) async-start(), calls=%async_computation.2 | async-start | bytes 1572864 | tf_op jit(solution)/shard_map/all_gather | solution.py:21
  93.1 5.0 %collective-permute-start = (s32[4,2]{0,1:T(2,128)S(1)}, s32[4,2]{0,1:T(2,128)S(1)}, u32[]{:S(2)}, u32[]{:S(2)}) collective-permute-start(s32[4,2]{0,1:T(2,128)S(1)} %bitcast.94), channel_id=1, source_target_pairs={{0,1},{2,3},{4,5},{6,7},{8,9},{10,11},{12,13},{14,15},{16,17},{18,... | collective-permute-start | bytes 104 | tf_op jit(solution)/shard_map/ppermute | solution.py:17
  105.4 3.1 %copy-start = (bf16[12,128,576]{1,2,0:T(8,128)(2,1)S(1)}, bf16[12,128,576]{1,2,0:T(8,128)(2,1)}, u32[]{:S(2)}) copy-start(bf16[12,128,576]{1,2,0:T(8,128)(2,1)} %get-tuple-element.88) | copy-start | bytes 5308420 | tf_op jit(solution)/shard_map/cond
  113.3 1.0 copy-start.2
  113.3 2.6 %copy-start.3 = (pred[4,4]{1,0:T(4,128)(4,1)S(1)}, pred[4,4]{1,0:T(4,128)(4,1)}, u32[]{:S(2)}) copy-start(pred[4,4]{1,0:T(4,128)(4,1)} %iota_compare_fusion.2) | copy-start | bytes 52 | tf_op jit(solution)/shard_map/cond
Sparse Core Ops, SparseCore 0:
  124.0 18.9 all-gather.6
where the time goes:
time: 153 us; the launch traced here: 152 us
  blocking collectives  65.1 us (43%)
  local copies, waits for them, and re-layouts  25.6 us (17%)
  waiting for transfers between devices  20.2 us (13%)
  between operations  13.6 us (9%)
  other arithmetic  11.2 us (7%)
  matrix products  10.3 us (7%)
  starting transfers between devices  5.83 us (4%)
    all_to_all x1, blocking collectives, local(): lax.all_to_all(packed, 'seq', split_axis=0, concat_axis=0, tiled=True)  58.4 us
    all_gather x1, waiting for transfers between devices, combined_all(): pieces = jax.tree.map(lambda part: lax.all_gather(part, axis), value)  12.3 us
    gather x2, local copies, waits for them, and re-layouts, pack_pieces(): fresh[token_index]  12.3 us
    all_gather x2, blocking collectives, combined_all(): pieces = jax.tree.map(lambda part: lax.all_gather(part, axis), value)  6.72 us
    dot_general x2, matrix products, part_softmax(): jnp.einsum('bhk,bkv->bhv', weights.astype(jnp.bfloat16), key_rows[:, :, :...  5.5 us
    another operation x2, local copies, waits for them, and re-layouts  4.84 us
    all_to_all x1, waiting for transfers between devices, local(): lax.all_to_all(packed_meta, 'seq', split_axis=0, concat_axis=0, tiled=True)  4.26 us
    ppermute x2, waiting for transfers between devices, passed_along(): return lax.ppermute(block, axis, route)  3.69 us
  transfers between devices with their start and end apart: 4, of which 3 were waited for; matrix products, arithmetic and copies ran while one was open for 1% of the time, Pallas kernels for 0%

commit v1 on v0

v1 whole, which is shorter than its diff:
```python
import functools

import jax
import jax.numpy as jnp
import numpy as np
from jax import lax
from jax.experimental import pallas as pl
from jax.experimental.pallas import tpu as pltpu
from jax.sharding import PartitionSpec as P

FRESH_DEV = 1024
SOFT_SCALE = 192.0 ** (-0.5)
MASKED = -1e30
NORM_EPSILON = 1e-06
GROUP = 4
MESH = pl.DeviceIdType.MESH


def stats_block(out, row_max, row_total, slot):
    lane = lax.broadcasted_iota(jnp.int32, (out.shape[0], 128), 1)
    return jnp.where(lane == 0, row_max, jnp.where(lane == 1, row_total, slot))


def kernel(
    n_seq, n_tp, pool_ref, q_ref, table_ref, res_ref, len_ref, owner_ref, slot_ref, pos_ref,
    gain_ref, freq_ref, out_ref,
    pool, fresh, q_in, q_out, meta_in, meta_out, weights, piece_out, piece_in, res_out, res_in,
    pool_sem, meta_send, meta_recv, q_send, q_recv, piece_send, piece_recv, res_send, res_recv,
):
    pages, width, page = pool.shape
    rows, heads, _ = q_ref.shape
    latent = gain_ref.shape[1]
    half = (width - latent) // 2
    share = heads // n_tp
    fresh_pages = FRESH_DEV // page
    seq = lax.axis_index("seq")
    tp = lax.axis_index("tp")
    section = lax.axis_index("section")
    barrier = pltpu.get_barrier_semaphore()

    def at(s, t, c):
        return {"seq": s, "tp": t, "section": c}

    def meta_copy(peer, own):
        return pltpu.make_async_remote_copy(
            meta_out.at[peer], meta_in.at[own], meta_send.at[peer], meta_recv.at[own],
            device_id=at(peer, tp, 0), device_id_type=MESH,
        )

    def q_copy(peer, own):
        return pltpu.make_async_remote_copy(
            q_out.at[peer], q_in.at[own], q_send.at[peer], q_recv.at[own],
            device_id=at(peer, tp, 0), device_id_type=MESH,
        )

    def piece_copy(d, t, own):
        return pltpu.make_async_remote_copy(
            piece_out.at[d, t], piece_in.at[own], piece_send.at[d * n_tp + t], piece_recv.at[own],
            device_id=at(d, t, 1), device_id_type=MESH,
        )

    def res_copy(t, own):
        return pltpu.make_async_remote_copy(
            res_out.at[t], res_in.at[own], res_send.at[t], res_recv.at[own],
            device_id=at(seq, t, 1), device_id_type=MESH,
        )

    @pl.when(section == 0)
    def prefill():
        raw_copy = pltpu.make_async_copy(
            pool_ref.at[pl.ds(0, fresh_pages)], pool.at[pl.ds(0, fresh_pages)], pool_sem
        )
        raw_copy.start()
        for k in range(1, n_seq):
            pl.semaphore_signal(
                barrier, inc=1, device_id=at(lax.rem(seq + k, n_seq), tp, 0), device_id_type=MESH
            )

        lengths = [len_ref[0, 0, k] for k in range(n_seq)]
        begins = [jnp.int32(0)]
        for k in range(n_seq - 1):
            begins.append(begins[-1] + lengths[k])

        def of_owner(d, values):
            total = jnp.int32(0)
            for k in range(n_seq):
                total = total + jnp.where(owner_ref[0, 0, k] == d, values[k], 0)
            return total

        slots = [slot_ref[0, 0, k] for k in range(n_seq)]
        owner_begin = [of_owner(d, begins) for d in range(n_seq)]
        owner_len = [of_owner(d, lengths) for d in range(n_seq)]
        owner_slot = [of_owner(d, slots) for d in range(n_seq)]
        for d in range(n_seq):
            meta_out[d] = jnp.full(meta_out.shape[1:], owner_slot[d], jnp.int32)

        pl.semaphore_wait(barrier, n_seq - 1 + n_seq * n_tp)
        for k in range(1, n_seq):
            meta_copy(lax.rem(seq + k, n_seq), seq).start()

        turns = []
        for j in range(fresh_pages):
            token = lax.broadcasted_iota(jnp.int32, (1, page), 1) + j * page
            shift = jnp.zeros((1, page), jnp.int32)
            for k in range(n_seq):
                live = (token >= begins[k]) & (token < begins[k] + lengths[k])
                shift = jnp.where(live, pos_ref[0, 0, k] - begins[k], shift)
            angles = (token + shift).astype(jnp.float32) * freq_ref[...]
            turns.append((jnp.cos(angles), jnp.sin(angles)))

        for k in range(1, n_seq):
            peer = lax.rem(seq + k, n_seq)
            meta_copy(peer, peer).wait_recv()
            wanted = meta_in[peer][0:1, 0:1]
            picked = q_ref[0].astype(jnp.float32)
            for r in range(1, rows):
                picked = jnp.where(wanted == r, q_ref[r].astype(jnp.float32), picked)
            q_out[peer] = picked.astype(jnp.bfloat16)
            q_copy(peer, seq).start()
        own_slot = meta_out[seq][0:1, 0:1]
        picked = q_ref[0].astype(jnp.float32)
        for r in range(1, rows):
            picked = jnp.where(own_slot == r, q_ref[r].astype(jnp.float32), picked)
        q_in[seq] = picked.astype(jnp.bfloat16)

        raw_copy.wait()
        gain = jnp.broadcast_to(gain_ref[...], (page, latent)).T
        for j in range(fresh_pages):
            x = pool[j, :latent].astype(jnp.float32)
            mean = jnp.mean(x * x, axis=0, keepdims=True)
            columns = slice(j * page, (j + 1) * page)
            normed = x * lax.rsqrt(mean + NORM_EPSILON) * gain
            fresh[:latent, columns] = normed.astype(jnp.bfloat16)
            y = pool[j, latent:].astype(jnp.float32)
            a, b = y[:half], y[half:]
            cosine, sine = turns[j]
            turned = jnp.concatenate([a * cosine - b * sine, b * cosine + a * sine], axis=0)
            fresh[latent:, columns] = turned.astype(jnp.bfloat16)

        out_ref[...] = jnp.zeros_like(out_ref)
        for k in range(1, n_seq):
            peer = lax.rem(seq + k, n_seq)
            q_copy(peer, peer).wait_recv()

        tokens = lax.broadcasted_iota(jnp.int32, (1, FRESH_DEV), 1)
        for first in range(0, n_seq, GROUP):
            scores = (
                jnp.dot(
                    q_in[first : first + GROUP].reshape(GROUP * heads, width),
                    fresh[...],
                    preferred_element_type=jnp.float32,
                )
                * SOFT_SCALE
            )
            stats = []
            for i in range(GROUP):
                d = first + i
                live = (tokens >= owner_begin[d]) & (tokens < owner_begin[d] + owner_len[d])
                part = jnp.where(live, scores[i * heads : (i + 1) * heads], MASKED)
                row_max = jnp.max(part, axis=1, keepdims=True)
                e = jnp.where(live, jnp.exp(part - row_max), 0.0)
                row_total = jnp.sum(e, axis=1, keepdims=True)
                weights[i * heads : (i + 1) * heads] = e.astype(jnp.bfloat16)
                stats.append(
                    stats_block(e, row_max, row_total, owner_slot[d].astype(jnp.float32))
                )
            for i in range(GROUP):
                d = first + i
                part_out = lax.dot_general(
                    weights[i * heads : (i + 1) * heads], fresh[:latent],
                    (((1,), (1,)), ((), ())), preferred_element_type=jnp.float32,
                )
                for t in range(n_tp):
                    mine = slice(t * share, (t + 1) * share)
                    piece_out[d, t, :, :latent] = part_out[mine]
                    piece_out[d, t, :, latent:] = stats[i][mine]
                    piece_copy(d, t, seq * n_tp + tp).start()

        for k in range(1, n_seq):
            peer = lax.rem(seq + k, n_seq)
            meta_copy(peer, peer).wait_send()
            q_copy(peer, peer).wait_send()
        for d in range(n_seq):
            for t in range(n_tp):
                piece_copy(d, t, 0).wait_send()

    @pl.when(section == 1)
    def decode():
        pool_copy = pltpu.make_async_copy(pool_ref, pool, pool_sem)
        pool_copy.start()
        for s in range(n_seq):
            for t in range(n_tp):
                pl.semaphore_signal(barrier, inc=1, device_id=at(s, t, 0), device_id_type=MESH)
        for k in range(1, n_tp):
            pl.semaphore_signal(
                barrier, inc=1, device_id=at(seq, lax.rem(tp + k, n_tp), 1), device_id_type=MESH
            )
        pool_copy.wait()
        most = table_ref.shape[2]
        tokens = lax.broadcasted_iota(jnp.int32, (1, most * page), 1)
        for r in range(rows):
            keys = jnp.concatenate([pool[table_ref[r, 0, j]] for j in range(most)], axis=1)
            scores = jnp.dot(q_ref[r], keys, preferred_element_type=jnp.float32) * SOFT_SCALE
            live = tokens < res_ref[r, 0]
            scores = jnp.where(live, scores, MASKED)
            row_max = jnp.max(scores, axis=1, keepdims=True)
            e = jnp.where(live, jnp.exp(scores - row_max), 0.0)
            row_total = jnp.sum(e, axis=1, keepdims=True)
            part_out = lax.dot_general(
                e.astype(jnp.bfloat16), keys[:latent],
                (((1,), (1,)), ((), ())), preferred_element_type=jnp.float32,
            )
            stats = stats_block(e, row_max, row_total, 0.0)
            for t in range(n_tp):
                mine = slice(t * share, (t + 1) * share)
                res_out[t, r, :, :latent] = part_out[mine]
                res_out[t, r, :, latent:] = stats[mine]
        if n_tp > 1:
            pl.semaphore_wait(barrier, n_tp - 1)
        for k in range(1, n_tp):
            res_copy(lax.rem(tp + k, n_tp), tp).start()
        res_in[tp] = res_out[tp]
        for k in range(1, n_tp):
            peer = lax.rem(tp + k, n_tp)
            res_copy(peer, peer).wait_recv()
        for p in range(n_seq * n_tp):
            piece_copy(0, 0, p).wait_recv()

        piece_max = [piece_in[p, :, latent : latent + 1] for p in range(n_seq * n_tp)]
        piece_total = [piece_in[p, :, latent + 1 : latent + 2] for p in range(n_seq * n_tp)]
        piece_slot = [piece_in[p, :, latent + 2 : latent + 3] for p in range(n_seq * n_tp)]
        for r in range(rows):
            parts = [res_in[t, r, :, latent : latent + 1] for t in range(n_tp)]
            parts += [
                jnp.where(piece_slot[p] == float(r), piece_max[p], MASKED)
                for p in range(n_seq * n_tp)
            ]
            joint = functools.reduce(jnp.maximum, parts)
            total = jnp.zeros((share, 1), jnp.float32)
            out = jnp.zeros((share, latent), jnp.float32)
            for t in range(n_tp):
                scale = jnp.exp(parts[t] - joint)
                total += res_in[t, r, :, latent + 1 : latent + 2] * scale
                out += res_in[t, r, :, :latent] * scale
            for p in range(n_seq * n_tp):
                scale = jnp.where(
                    piece_slot[p] == float(r), jnp.exp(parts[n_tp + p] - joint), 0.0
                )
                total += piece_total[p] * scale
                out += piece_in[p, :, :latent] * scale
            out_ref[0, r] = (out / total).astype(jnp.bfloat16)
        for k in range(1, n_tp):
            res_copy(lax.rem(tp + k, n_tp), tp).wait_send()


def local(
    n_seq, n_tp,
    page_pool, queries, block_table, res_len, piece_len, piece_owner, piece_slot, piece_pos, kv_gain
):
    pages, page, width = page_pool.shape
    rows, heads, _ = queries.shape
    latent = kv_gain.shape[0]
    half = (width - latent) // 2
    share = heads // n_tp
    freq = np.float64(10000.0) ** (-np.arange(half) / half)
    freq = jnp.asarray(np.broadcast_to(freq.astype(np.float32)[:, None], (half, page)))
    vmem = pl.BlockSpec(memory_space=pltpu.VMEM)
    smem = pl.BlockSpec(memory_space=pltpu.SMEM)
    parts = n_seq * n_tp
    return pl.pallas_call(
        functools.partial(kernel, n_seq, n_tp),
        out_shape=jax.ShapeDtypeStruct((1, rows, share, latent), jnp.bfloat16),
        in_specs=[pl.BlockSpec(memory_space=pl.ANY), vmem] + [smem] * 6 + [vmem, vmem],
        out_specs=vmem,
        scratch_shapes=[
            pltpu.VMEM((pages, width, page), jnp.bfloat16),
            pltpu.VMEM((width, FRESH_DEV), jnp.bfloat16),
            pltpu.VMEM((n_seq, heads, width), jnp.bfloat16),
            pltpu.VMEM((n_seq, heads, width), jnp.bfloat16),
            pltpu.VMEM((n_seq, 8, 128), jnp.int32),
            pltpu.VMEM((n_seq, 8, 128), jnp.int32),
            pltpu.VMEM((GROUP * heads, FRESH_DEV), jnp.bfloat16),
            pltpu.VMEM((n_seq, n_tp, share, latent + 128), jnp.float32),
            pltpu.VMEM((parts, share, latent + 128), jnp.float32),
            pltpu.VMEM((n_tp, rows, share, latent + 128), jnp.float32),
            pltpu.VMEM((n_tp, rows, share, latent + 128), jnp.float32),
            pltpu.SemaphoreType.DMA,
            pltpu.SemaphoreType.DMA((n_seq,)),
            pltpu.SemaphoreType.DMA((n_seq,)),
            pltpu.SemaphoreType.DMA((n_seq,)),
            pltpu.SemaphoreType.DMA((n_seq,)),
            pltpu.SemaphoreType.DMA((parts,)),
            pltpu.SemaphoreType.DMA((parts,)),
            pltpu.SemaphoreType.DMA((n_tp,)),
            pltpu.SemaphoreType.DMA((n_tp,)),
        ],
        compiler_params=pltpu.CompilerParams(
            collective_id=0, has_side_effects=True, vmem_limit_bytes=48 * 1024 * 1024
        ),
    )(
        jnp.swapaxes(page_pool, 1, 2), queries, block_table, res_len, piece_len, piece_owner,
        piece_slot, piece_pos, kv_gain[None], freq,
    )


def solution(mesh):
    return jax.shard_map(
        functools.partial(local, mesh.shape["seq"], mesh.shape["tp"]),
        mesh=mesh,
        in_specs=(
            P(("groups", "seq", "tp", "section"), None, None),
            P(("groups", "seq"), None, None),
            P(("groups", "seq"), "tp", None),
            P(("groups", "seq"), "tp"),
            P(("groups", "seq"), "tp", None),
            P(("groups", "seq"), "tp", None),
            P(("groups", "seq"), "tp", None),
            P(("groups", "seq"), "tp", None),
            P(),
        ),
        out_specs=P("section", ("groups", "seq"), "tp", None),
        check_vma=False,
    )
```

time: 153 us -> 35 us (0.23)
  the two profiles are of different devices: /device:TPU:1 before, /device:TPU:31 now
where the time goes in v1:
time: 35 us; the launch traced here: 34.7 us
  Pallas kernels  26.1 us (75%)
  local copies, waits for them, and re-layouts  8.55 us (24%)
    pallas_call x1, Pallas kernels, local(): pl.pallas_call(functools.partial(kernel, n_seq, n_tp), out_shape=jax.Shap...  26.1 us
    unnamed x18, local copies, waits for them, and re-layouts  7.83 us
    another operation x1, local copies, waits for them, and re-layouts  0.72 us

profile of v1, /device:TPU:31, one launch (start us, length us, event | category | flops | bytes accessed | tf_op | source)
XLA Modules:
  0.0 34.7 jit_solution(5416917492952271888)
XLA Ops:
  0.0 0.7 %copy.11.res_ref = s32[4,1]{1,0:T(4,128)S(1)} copy(s32[4,1]{0,1:T(1,128)} %param.13) | data formatting | bytes 32 | tf_op args[3]
  0.7 0.7 %jit_solution_.3.freq_ref = f32[32,128]{1,0:T(8,128)S(1)} broadcast(f32[32]{0:T(128)} %constant.2.clone), dimensions={0} | broadcast | bytes 16512 | tf_op jit(solution)
  1.5 0.0 copy-start
  1.5 1.5 %copy-done = bf16[12,128,576]{1,2,0:T(8,128)(2,1)S(1)} copy-done((bf16[12,128,576]{1,2,0:T(8,128)(2,1)S(1)}, bf16[12,128,576]{1,2,0:T(8,128)(2,1)}, u32[]{:S(2)}) %copy-start) | copy-done | bytes 1769496
  2.9 0.0 copy-start.1
  2.9 1.0 %copy-done.1 = bf16[4,64,576]{2,1,0:T(8,128)(2,1)S(1)} copy-done((bf16[4,64,576]{2,1,0:T(8,128)(2,1)S(1)}, bf16[4,64,576]{2,1,0:T(8,128)(2,1)}, u32[]{:S(2)}) %copy-start.1) | copy-done | bytes 294936
  3.9 0.0 copy-start.2
  3.9 0.7 %copy-done.2 = s32[4,1,4]{2,1,0:T(1,128)S(1)} copy-done((s32[4,1,4]{2,1,0:T(1,128)S(1)}, s32[4,1,4]{2,1,0:T(1,128)}, u32[]{:S(2)}) %copy-start.2) | copy-done | bytes 88
  4.6 0.0 copy-start.3
  4.6 0.7 %copy-done.3 = f32[512]{0:T(512)S(1)} copy-done((f32[512]{0:T(512)S(1)}, f32[512]{0:T(512)}, u32[]{:S(2)}) %copy-start.3) | copy-done | bytes 2072
  5.3 0.0 copy-start.4
  5.3 0.7 %copy-done.4 = s32[1,1,4]{2,1,0:T(1,128)S(1)} copy-done((s32[1,1,4]{2,1,0:T(1,128)S(1)}, s32[1,1,4]{2,1,0:T(1,128)}, u32[]{:S(2)}) %copy-start.4) | copy-done | bytes 40
  5.9 0.0 copy-start.5
  5.9 0.7 %copy-done.5 = s32[1,1,4]{2,1,0:T(1,128)S(1)} copy-done((s32[1,1,4]{2,1,0:T(1,128)S(1)}, s32[1,1,4]{2,1,0:T(1,128)}, u32[]{:S(2)}) %copy-start.5) | copy-done | bytes 40
  6.6 0.0 copy-start.6
  6.6 0.7 %copy-done.6 = s32[1,1,4]{2,1,0:T(1,128)S(1)} copy-done((s32[1,1,4]{2,1,0:T(1,128)S(1)}, s32[1,1,4]{2,1,0:T(1,128)}, u32[]{:S(2)}) %copy-start.6) | copy-done | bytes 40
  7.2 0.0 copy-start.7
  7.3 0.7 %copy-done.7 = s32[1,1,4]{2,1,0:T(1,128)S(1)} copy-done((s32[1,1,4]{2,1,0:T(1,128)S(1)}, s32[1,1,4]{2,1,0:T(1,128)}, u32[]{:S(2)}) %copy-start.7) | copy-done | bytes 40
  7.9 26.1 %shard_map.100 = bf16[1,4,32,512]{3,2,1,0:T(8,128)(2,1)S(1)} custom-call(bf16[12,576,128]{2,1,0:T(8,128)(2,1)S(1)} %bitcast.2, bf16[4,64,576]{2,1,0:T(8,128)(2,1)S(1)} %copy-done.1, s32[4,1,4]{2,1,0:T(1,128)S(1)} %copy-done.2, s32[4,1]{1,0:T(4,128)S(1)} %copy.11.res_ref, s32[1,1,4]{2,1,0:T(1,128)S(1)} %copy-done.4, s32[1,1,4]{2,1,0:T(1,128)S(1)} %copy-done.5, ...), custom_call_target="tpu_custom_call" | custom-call | tf_op jit(solution)/shard_map/pallas_call | solution.py:270
  34.0 0.7 %copy.13 = bf16[1,4,32,512]{3,2,1,0:T(8,128)(2,1)} copy(bf16[1,4,32,512]{3,2,1,0:T(8,128)(2,1)S(1)} %shard_map.100) | data formatting | bytes 262144
Async XLA Ops:
  1.5 1.5 %copy-start = (bf16[12,128,576]{1,2,0:T(8,128)(2,1)S(1)}, bf16[12,128,576]{1,2,0:T(8,128)(2,1)}, u32[]{:S(2)}) copy-start(bf16[12,128,576]{1,2,0:T(8,128)(2,1)} %param.10) | copy-start | bytes 5308420
  2.9 1.0 %copy-start.1 = (bf16[4,64,576]{2,1,0:T(8,128)(2,1)S(1)}, bf16[4,64,576]{2,1,0:T(8,128)(2,1)}, u32[]{:S(2)}) copy-start(bf16[4,64,576]{2,1,0:T(8,128)(2,1)} %q_ref.1) | copy-start | bytes 884740
  3.9 0.7 %copy-start.2 = (s32[4,1,4]{2,1,0:T(1,128)S(1)}, s32[4,1,4]{2,1,0:T(1,128)}, u32[]{:S(2)}) copy-start(s32[4,1,4]{2,1,0:T(1,128)} %table_ref.1) | copy-start | bytes 196
  4.6 0.7 %copy-start.3 = (f32[512]{0:T(512)S(1)}, f32[512]{0:T(512)}, u32[]{:S(2)}) copy-start(f32[512]{0:T(512)} %param.18) | copy-start | bytes 6148
  5.3 0.7 %copy-start.4 = (s32[1,1,4]{2,1,0:T(1,128)S(1)}, s32[1,1,4]{2,1,0:T(1,128)}, u32[]{:S(2)}) copy-start(s32[1,1,4]{2,1,0:T(1,128)} %len_ref.1) | copy-start | bytes 52
  5.9 0.7 %copy-start.5 = (s32[1,1,4]{2,1,0:T(1,128)S(1)}, s32[1,1,4]{2,1,0:T(1,128)}, u32[]{:S(2)}) copy-start(s32[1,1,4]{2,1,0:T(1,128)} %owner_ref.1) | copy-start | bytes 52
  6.6 0.7 %copy-start.6 = (s32[1,1,4]{2,1,0:T(1,128)S(1)}, s32[1,1,4]{2,1,0:T(1,128)}, u32[]{:S(2)}) copy-start(s32[1,1,4]{2,1,0:T(1,128)} %slot_ref.1) | copy-start | bytes 52
  7.2 0.7 %copy-start.7 = (s32[1,1,4]{2,1,0:T(1,128)S(1)}, s32[1,1,4]{2,1,0:T(1,128)}, u32[]{:S(2)}) copy-start(s32[1,1,4]{2,1,0:T(1,128)} %pos_ref.1) | copy-start | bytes 52

commit v2 on v1

v2 whole, which is shorter than its diff:
```python
import functools

import jax
import jax.numpy as jnp
import numpy as np
from jax import lax
from jax.experimental import pallas as pl
from jax.experimental.pallas import tpu as pltpu
from jax.sharding import PartitionSpec as P

FRESH_DEV = 1024
SOFT_SCALE = 192.0 ** (-0.5)
MASKED = -1e30
NORM_EPSILON = 1e-06
GROUP = 2
MESH = pl.DeviceIdType.MESH


def stats_rows(row_max, row_total, slot):
    lane = lax.broadcasted_iota(jnp.int32, (row_max.shape[0], 128), 1)
    block = jnp.where(lane == 0, row_max, jnp.where(lane == 1, row_total, slot))
    return block.T[:8]


def cos_sin(angles):
    turns = jnp.floor(angles * (2.0 / np.pi) + 0.5)
    rest = angles - turns * 1.5703125
    rest = rest - turns * 4.837512969970703125e-4
    rest = rest - turns * 7.54978995489188216e-8
    square = rest * rest
    sine = rest + rest * square * (
        -1.6666654611e-1 + square * (8.3321608736e-3 + square * -1.9515295891e-4)
    )
    cosine = (
        1.0
        - 0.5 * square
        + square * square
        * (4.166664568298827e-2 + square * (-1.388731625493765e-3 + square * 2.443315711809948e-5))
    )
    quarter = turns.astype(jnp.int32) & 3
    odd = (quarter & 1) == 1
    cos_value = jnp.where(odd, sine, cosine)
    sin_value = jnp.where(odd, cosine, sine)
    cos_value = jnp.where((quarter == 1) | (quarter == 2), -cos_value, cos_value)
    sin_value = jnp.where(quarter >= 2, -sin_value, sin_value)
    return cos_value, sin_value


def kernel(
    n_seq, n_tp, pool_hbm, q_hbm, table_hbm, res_hbm, len_hbm, owner_hbm, slot_hbm, pos_hbm,
    gain_hbm, out_ref,
    q_ref, table_ref, res_ref, len_ref, owner_ref, slot_ref, pos_ref, gain_ref, load_sem,
    pool, fresh, q_in, q_out, meta_in, meta_out, piece_out, piece_in, res_out, res_in, res_sum,
    pool_sem, meta_send, meta_recv, q_send, q_recv, piece_send, piece_recv, res_send, res_recv,
):
    pages, width, page = pool.shape
    rows, heads, _ = q_ref.shape
    latent = gain_ref.shape[1]
    half = (width - latent) // 2
    share = heads // n_tp
    fresh_pages = FRESH_DEV // page
    chunks = latent // 128
    seq = lax.axis_index("seq")
    tp = lax.axis_index("tp")
    section = lax.axis_index("section")
    barrier = pltpu.get_barrier_semaphore()
    order = [lax.rem((seq // 2) * 2 + 2 + i, n_seq) for i in range(n_seq)]
    peers = order[: n_seq - 2] + [(seq // 2) * 2 + 1 - lax.rem(seq, 2)]

    loads = [
        pltpu.make_async_copy(source, target, load_sem.at[i])
        for i, (source, target) in enumerate(
            [
                (len_hbm, len_ref), (owner_hbm, owner_ref), (slot_hbm, slot_ref),
                (pos_hbm, pos_ref), (table_hbm, table_ref), (res_hbm, res_ref),
                (q_hbm, q_ref), (gain_hbm, gain_ref),
            ]
        )
    ]
    for load in loads:
        load.start()

    def at(s, t, c):
        return {"seq": s, "tp": t, "section": c}

    def meta_copy(peer, own):
        return pltpu.make_async_remote_copy(
            meta_out.at[peer], meta_in.at[own], meta_send.at[peer], meta_recv.at[own],
            device_id=at(peer, tp, 0), device_id_type=MESH,
        )

    def q_copy(peer, own):
        return pltpu.make_async_remote_copy(
            q_out.at[peer], q_in.at[own], q_send.at[peer], q_recv.at[own],
            device_id=at(peer, tp, 0), device_id_type=MESH,
        )

    def piece_copy(i, t, own):
        return pltpu.make_async_remote_copy(
            piece_out.at[i, t], piece_in.at[own], piece_send.at[i * n_tp + t], piece_recv.at[own],
            device_id=at(order[i], t, 1), device_id_type=MESH,
        )

    def res_copy(t, own):
        return pltpu.make_async_remote_copy(
            res_out.at[t], res_in.at[own], res_send.at[t], res_recv.at[own],
            device_id=at(seq, t, 1), device_id_type=MESH,
        )

    @pl.when(section == 0)
    def prefill():
        raw_copy = pltpu.make_async_copy(
            pool_hbm.at[pl.ds(0, fresh_pages)], pool.at[pl.ds(0, fresh_pages)], pool_sem
        )
        raw_copy.start()
        for peer in peers:
            pl.semaphore_signal(barrier, inc=1, device_id=at(peer, tp, 0), device_id_type=MESH)
        for load in loads:
            load.wait()

        lengths = [len_ref[0, 0, k] for k in range(n_seq)]
        begins = [jnp.int32(0)]
        for k in range(n_seq - 1):
            begins.append(begins[-1] + lengths[k])

        def of_owner(d, values):
            total = jnp.int32(0)
            for k in range(n_seq):
                total = total + jnp.where(owner_ref[0, 0, k] == d, values[k], 0)
            return total

        slots = [slot_ref[0, 0, k] for k in range(n_seq)]
        owner_begin = [of_owner(d, begins) for d in order]
        owner_len = [of_owner(d, lengths) for d in order]
        owner_slot = [of_owner(d, slots) for d in order]
        for i, d in enumerate(order):
            meta_out[d] = jnp.full(meta_out.shape[1:], owner_slot[i], jnp.int32)

        pl.semaphore_wait(barrier, n_seq - 1 + n_seq * n_tp)
        for peer in peers:
            meta_copy(peer, seq).start()

        for peer in peers:
            meta_copy(peer, peer).wait_recv()
            wanted = meta_in[peer][0:1, 0:1]
            picked = q_ref[0].astype(jnp.float32)
            for r in range(1, rows):
                picked = jnp.where(wanted == r, q_ref[r].astype(jnp.float32), picked)
            q_out[peer] = picked.astype(jnp.bfloat16)
            q_copy(peer, seq).start()
        own_slot = meta_out[seq][0:1, 0:1]
        picked = q_ref[0].astype(jnp.float32)
        for r in range(1, rows):
            picked = jnp.where(own_slot == r, q_ref[r].astype(jnp.float32), picked)
        q_in[seq] = picked.astype(jnp.bfloat16)

        out_ref[...] = jnp.zeros_like(out_ref)
        raw_copy.wait()
        gain = jnp.broadcast_to(gain_ref[...], (page, latent)).T
        index = lax.broadcasted_iota(jnp.int32, (half, page), 0)
        freq = jnp.ones((half, page), jnp.float32)
        for i in range(1, half):
            freq = jnp.where(index == i, float(10000.0 ** (-i / half)), freq)
        for j in range(fresh_pages):
            x = pool[j, :latent].astype(jnp.float32)
            mean = jnp.mean(x * x, axis=0, keepdims=True)
            columns = slice(j * page, (j + 1) * page)
            normed = x * lax.rsqrt(mean + NORM_EPSILON) * gain
            fresh[:latent, columns] = normed.astype(jnp.bfloat16)
            y = pool[j, latent:].astype(jnp.float32)
            a, b = y[:half], y[half:]
            token = lax.broadcasted_iota(jnp.int32, (1, page), 1) + j * page
            shift = jnp.zeros((1, page), jnp.int32)
            for k in range(n_seq):
                live = (token >= begins[k]) & (token < begins[k] + lengths[k])
                shift = jnp.where(live, pos_ref[0, 0, k] - begins[k], shift)
            cosine, sine = cos_sin((token + shift).astype(jnp.float32) * freq)
            turned = jnp.concatenate([a * cosine - b * sine, b * cosine + a * sine], axis=0)
            fresh[latent:, columns] = turned.astype(jnp.bfloat16)

        out_ref[...] = jnp.zeros_like(out_ref)
        tokens = lax.broadcasted_iota(jnp.int32, (1, FRESH_DEV), 1)
        for first in range(0, n_seq, GROUP):
            for d in peers[first : first + GROUP]:
                q_copy(d, d).wait_recv()
            members = range(first, first + GROUP)
            wide = jnp.concatenate([q_in[order[i]] for i in members], axis=0)
            scores = jnp.dot(wide, fresh[...], preferred_element_type=jnp.float32) * SOFT_SCALE
            stats = []
            weights = []
            for i in members:
                live = (tokens >= owner_begin[i]) & (tokens < owner_begin[i] + owner_len[i])
                here = (i - first) * heads
                part = jnp.where(live, scores[here : here + heads], MASKED)
                row_max = jnp.max(part, axis=1, keepdims=True)
                e = jnp.where(live, jnp.exp(part - row_max), 0.0)
                row_total = jnp.sum(e, axis=1, keepdims=True)
                weights.append(e.astype(jnp.bfloat16))
                stats.append((row_max, row_total, owner_slot[i].astype(jnp.float32)))
            group_out = lax.dot_general(
                jnp.concatenate(weights, axis=0), fresh[:latent],
                (((1,), (1,)), ((), ())), preferred_element_type=jnp.float32,
            )
            for i in members:
                for t in range(n_tp):
                    here = (i - first) * heads + t * share
                    mine = slice(t * share, (t + 1) * share)
                    for c in range(chunks):
                        piece_out[i, t, c * share : (c + 1) * share] = group_out[
                            here : here + share, c * 128 : (c + 1) * 128
                        ]
                    row_max, row_total, slot = stats[i - first]
                    piece_out[i, t, chunks * share :, :share] = stats_rows(
                        row_max[mine], row_total[mine], slot
                    )
                    piece_copy(i, t, seq * n_tp + tp).start()

        for peer in peers:
            meta_copy(peer, peer).wait_send()
            q_copy(peer, peer).wait_send()
        for d in range(n_seq):
            for t in range(n_tp):
                piece_copy(d, t, 0).wait_send()

    @pl.when(section == 1)
    def decode():
        pool_copy = pltpu.make_async_copy(pool_hbm, pool, pool_sem)
        pool_copy.start()
        for s in range(n_seq):
            for t in range(n_tp):
                pl.semaphore_signal(barrier, inc=1, device_id=at(s, t, 0), device_id_type=MESH)
        for k in range(1, n_tp):
            pl.semaphore_signal(
                barrier, inc=1, device_id=at(seq, lax.rem(tp + k, n_tp), 1), device_id_type=MESH
            )
        for load in loads:
            load.wait()
        pool_copy.wait()
        most = table_ref.shape[2]
        tokens = lax.broadcasted_iota(jnp.int32, (1, most * page), 1)
        for r in range(rows):
            keys = jnp.concatenate([pool[table_ref[r, 0, j]] for j in range(most)], axis=1)
            scores = jnp.dot(q_ref[r], keys, preferred_element_type=jnp.float32) * SOFT_SCALE
            live = tokens < res_ref[0, r]
            scores = jnp.where(live, scores, MASKED)
            row_max = jnp.max(scores, axis=1, keepdims=True)
            e = jnp.where(live, jnp.exp(scores - row_max), 0.0)
            row_total = jnp.sum(e, axis=1, keepdims=True)
            part_out = lax.dot_general(
                e.astype(jnp.bfloat16), keys[:latent],
                (((1,), (1,)), ((), ())), preferred_element_type=jnp.float32,
            )
            for t in range(n_tp):
                mine = slice(t * share, (t + 1) * share)
                for c in range(chunks):
                    res_out[t, r, c * share : (c + 1) * share] = part_out[
                        mine, c * 128 : (c + 1) * 128
                    ]
                res_out[t, r, chunks * share :, :share] = stats_rows(
                    row_max[mine], row_total[mine], 0.0
                )
        if n_tp > 1:
            pl.semaphore_wait(barrier, n_tp - 1)
        for k in range(1, n_tp):
            res_copy(lax.rem(tp + k, n_tp), tp).start()
        res_in[tp] = res_out[tp]
        for k in range(1, n_tp):
            peer = lax.rem(tp + k, n_tp)
            res_copy(peer, peer).wait_recv()

        def columns(block):
            wide = jnp.concatenate([block[:, :share], jnp.zeros((8, 128 - share))], axis=1)
            turned = wide.T
            return turned[:share, 0:1], turned[:share, 1:2], turned[:share, 2:3]

        def joined(block, scale, sums):
            return [
                sums[c] + block[c * share : (c + 1) * share] * scale for c in range(chunks)
            ]

        tail = slice(chunks * share, chunks * share + 8)
        resident = []
        for r in range(rows):
            parts = [columns(res_in[t, r, tail]) for t in range(n_tp)]
            joint = functools.reduce(jnp.maximum, [part[0] for part in parts])
            total = jnp.zeros((share, 1), jnp.float32)
            sums = [jnp.zeros((share, 128), jnp.float32)] * chunks
            for t in range(n_tp):
                scale = jnp.exp(parts[t][0] - joint)
                total += parts[t][1] * scale
                sums = joined(res_in[t, r], scale, sums)
            for c in range(chunks):
                res_sum[r, c * share : (c + 1) * share] = sums[c]
            resident.append((joint, total))
        for p in range(n_seq * n_tp):
            piece_copy(0, 0, p).wait_recv()
        pieces = [columns(piece_in[p, tail]) for p in range(n_seq * n_tp)]
        for r in range(rows):
            row_max, row_total = resident[r]
            maxima = [
                jnp.where(slot == float(r), piece_max, MASKED) for piece_max, _, slot in pieces
            ]
            joint = functools.reduce(jnp.maximum, maxima, row_max)
            scale = jnp.exp(row_max - joint)
            total = row_total * scale
            sums = [res_sum[r, c * share : (c + 1) * share] * scale for c in range(chunks)]
            for p in range(n_seq * n_tp):
                scale = jnp.where(
                    pieces[p][2] == float(r), jnp.exp(maxima[p] - joint), 0.0
                )
                total += pieces[p][1] * scale
                sums = joined(piece_in[p], scale, sums)
            for c in range(chunks):
                out_ref[0, r, :, c * 128 : (c + 1) * 128] = (sums[c] / total).astype(jnp.bfloat16)
        for k in range(1, n_tp):
            res_copy(lax.rem(tp + k, n_tp), tp).wait_send()


def local(
    n_seq, n_tp,
    page_pool, queries, block_table, res_len, piece_len, piece_owner, piece_slot, piece_pos, kv_gain
):
    pages, page, width = page_pool.shape
    rows, heads, _ = queries.shape
    latent = kv_gain.shape[0]
    share = heads // n_tp
    packed = latent // 128 * share + 8
    vmem = pl.BlockSpec(memory_space=pltpu.VMEM)
    parts = n_seq * n_tp
    return pl.pallas_call(
        functools.partial(kernel, n_seq, n_tp),
        out_shape=jax.ShapeDtypeStruct((1, rows, share, latent), jnp.bfloat16),
        in_specs=[pl.BlockSpec(memory_space=pl.ANY)] * 9,
        out_specs=vmem,
        scratch_shapes=[
            pltpu.VMEM(queries.shape, jnp.bfloat16),
            pltpu.SMEM(block_table.shape, jnp.int32),
            pltpu.SMEM(res_len.shape[::-1], jnp.int32),
            pltpu.SMEM(piece_len.shape, jnp.int32),
            pltpu.SMEM(piece_len.shape, jnp.int32),
            pltpu.SMEM(piece_len.shape, jnp.int32),
            pltpu.SMEM(piece_len.shape, jnp.int32),
            pltpu.VMEM((1, latent), jnp.float32),
            pltpu.SemaphoreType.DMA((8,)),
            pltpu.VMEM((pages, width, page), jnp.bfloat16),
            pltpu.VMEM((width, FRESH_DEV), jnp.bfloat16),
            pltpu.VMEM((n_seq, heads, width), jnp.bfloat16),
            pltpu.VMEM((n_seq, heads, width), jnp.bfloat16),
            pltpu.VMEM((n_seq, 8, 128), jnp.int32),
            pltpu.VMEM((n_seq, 8, 128), jnp.int32),
            pltpu.VMEM((n_seq, n_tp, packed, 128), jnp.float32),
            pltpu.VMEM((parts, packed, 128), jnp.float32),
            pltpu.VMEM((n_tp, rows, packed, 128), jnp.float32),
            pltpu.VMEM((n_tp, rows, packed, 128), jnp.float32),
            pltpu.VMEM((rows, packed, 128), jnp.float32),
            pltpu.SemaphoreType.DMA,
            pltpu.SemaphoreType.DMA((n_seq,)),
            pltpu.SemaphoreType.DMA((n_seq,)),
            pltpu.SemaphoreType.DMA((n_seq,)),
            pltpu.SemaphoreType.DMA((n_seq,)),
            pltpu.SemaphoreType.DMA((parts,)),
            pltpu.SemaphoreType.DMA((parts,)),
            pltpu.SemaphoreType.DMA((n_tp,)),
            pltpu.SemaphoreType.DMA((n_tp,)),
        ],
        compiler_params=pltpu.CompilerParams(
            collective_id=0, has_side_effects=True, vmem_limit_bytes=56 * 1024 * 1024
        ),
    )(
        jnp.swapaxes(page_pool, 1, 2), queries, block_table, res_len.T, piece_len,
        piece_owner, piece_slot, piece_pos, kv_gain[None],
    )


def solution(mesh):
    return jax.shard_map(
        functools.partial(local, mesh.shape["seq"], mesh.shape["tp"]),
        mesh=mesh,
        in_specs=(
            P(("groups", "seq", "tp", "section"), None, None),
            P(("groups", "seq"), None, None),
            P(("groups", "seq"), "tp", None),
            P(("groups", "seq"), "tp"),
            P(("groups", "seq"), "tp", None),
            P(("groups", "seq"), "tp", None),
            P(("groups", "seq"), "tp", None),
            P(("groups", "seq"), "tp", None),
            P(),
        ),
        out_specs=P("section", ("groups", "seq"), "tp", None),
        check_vma=False,
    )
```

time: 35 us -> 24.6 us (0.70)
  the two profiles are of different devices: /device:TPU:31 before, /device:TPU:1 now
where the time goes in v2:
time: 24.6 us; the launch traced here: 24.2 us
  Pallas kernels  22.6 us (92%)
  local copies, waits for them, and re-layouts  1.57 us (6%)
    pallas_call x1, Pallas kernels, local(): pl.pallas_call(functools.partial(kernel, n_seq, n_tp), out_shape=jax.Shap...  22.6 us
    unnamed x1, local copies, waits for them, and re-layouts  1.57 us

profile of v2, /device:TPU:1, one launch (start us, length us, event | category | flops | bytes accessed | tf_op | source)
XLA Modules:
  0.0 24.2 jit_solution(8549042007642155525)
XLA Ops:
  0.0 22.6 %shard_map.91 = bf16[1,4,32,512]{3,2,1,0:T(8,128)(2,1)} custom-call(bf16[12,576,128]{2,1,0:T(8,128)(2,1)} %bitcast.3, bf16[4,64,576]{2,1,0:T(8,128)(2,1)} %q_hbm.1, s32[4,1,4]{2,1,0:T(1,128)} %table_hbm.1, s32[1,4]{1,0:T(1,128)} %bitcast.5, s32[1,1,4]{2,1,0:T(1,128)} %len_hbm.1, s32[1,1,4]{2,1,0:T(1,128)} %owner_hbm.1, s32[1,1,4]{2,1,0:T(1,128)} %slot_hbm.1, ...), custom_call_target="tpu_custom_call" | custom-call | tf_op jit(solution)/shard_map/pallas_call | solution.py:330
  22.6 1.6 %copy.11 = bf16[1,4,32,512]{3,2,1,0:T(8,128)(2,1)} copy(bf16[1,4,32,512]{3,2,1,0:T(8,128)(2,1)} %shard_map.91) | data formatting | bytes 262144

commit v3 on v2

--- a/solution.py
+++ b/solution.py
@@ -13,12 +13,15 @@
 MASKED = -1e30
 NORM_EPSILON = 1e-06
 GROUP = 2
+STEPS = 32700.0
 MESH = pl.DeviceIdType.MESH
 
 
-def stats_rows(row_max, row_total, slot):
+def stats_rows(row_max, row_total, slot, step):
     lane = lax.broadcasted_iota(jnp.int32, (row_max.shape[0], 128), 1)
-    block = jnp.where(lane == 0, row_max, jnp.where(lane == 1, row_total, slot))
+    block = jnp.where(
+        lane == 0, row_max, jnp.where(lane == 1, row_total, jnp.where(lane == 2, slot, step))
+    )
     return block.T[:8]
 
 
@@ -50,8 +53,9 @@
     n_seq, n_tp, pool_hbm, q_hbm, table_hbm, res_hbm, len_hbm, owner_hbm, slot_hbm, pos_hbm,
     gain_hbm, out_ref,
     q_ref, table_ref, res_ref, len_ref, owner_ref, slot_ref, pos_ref, gain_ref, load_sem,
-    pool, fresh, q_in, q_out, meta_in, meta_out, piece_out, piece_in, res_out, res_in, res_sum,
-    pool_sem, meta_send, meta_recv, q_send, q_recv, piece_send, piece_recv, res_send, res_recv,
+    pool, fresh, q_in, q_out, meta_in, meta_out, piece_out, piece_in, stat_out, stat_in, scales, res_out, res_in, res_sum,
+    pool_sem, meta_send, meta_recv, q_send, q_recv, piece_send, piece_recv, stat_send, stat_recv,
+    res_send, res_recv,
 ):
     pages, width, page = pool.shape
     rows, heads, _ = q_ref.shape
@@ -98,6 +102,12 @@
     def piece_copy(i, t, own):
         return pltpu.make_async_remote_copy(
             piece_out.at[i, t], piece_in.at[own], piece_send.at[i * n_tp + t], piece_recv.at[own],
+            device_id=at(order[i], t, 1), device_id_type=MESH,
+        )
+
+    def stat_copy(i, t, own):
+        return pltpu.make_async_remote_copy(
+            stat_out.at[i, t], stat_in.at[own], stat_send.at[i * n_tp + t], stat_recv.at[own],
             device_id=at(order[i], t, 1), device_id_type=MESH,
         )
 
@@ -201,18 +211,29 @@
                 jnp.concatenate(weights, axis=0), fresh[:latent],
                 (((1,), (1,)), ((), ())), preferred_element_type=jnp.float32,
             )
+            step = jnp.maximum(jnp.max(jnp.abs(group_out), axis=1, keepdims=True), 1e-30) / STEPS
+            for i in members:
+                row_max, row_total, slot = stats[i - first]
+                here = (i - first) * heads
+                for t in range(n_tp):
+                    mine = slice(t * share, (t + 1) * share)
+                    stat_out[i, t, :, :share] = stats_rows(
+                        row_max[mine], row_total[mine], slot,
+                        step[here + t * share : here + (t + 1) * share],
+                    )
+                    stat_copy(i, t, seq * n_tp + tp).start()
+            counted = jnp.floor(group_out * (1.0 / step) + 0.5)
             for i in members:
                 for t in range(n_tp):
                     here = (i - first) * heads + t * share
-                    mine = slice(t * share, (t + 1) * share)
-                    for c in range(chunks):
-                        piece_out[i, t, c * share : (c + 1) * share] = group_out[
-                            here : here + share, c * 128 : (c + 1) * 128
-                        ]
-                    row_max, row_total, slot = stats[i - first]
-                    piece_out[i, t, chunks * share :, :share] = stats_rows(
-                        row_max[mine], row_total[mine], slot
+                    stacked = jnp.concatenate(
+                        [
+                            counted[here : here + share, c * 128 : (c + 1) * 128]
+                            for c in range(chunks)
+                        ],
+                        axis=0,
                     )
+                    piece_out[i, t] = stacked.astype(jnp.int32).astype(jnp.int16)
                     piece_copy(i, t, seq * n_tp + tp).start()
 
         for peer in peers:
@@ -221,6 +242,7 @@
         for d in range(n_seq):
             for t in range(n_tp):
                 piece_copy(d, t, 0).wait_send()
+                stat_copy(d, t, 0).wait_send()
 
     @pl.when(section == 1)
     def decode():
@@ -257,7 +279,7 @@
                         mine, c * 128 : (c + 1) * 128
                     ]
                 res_out[t, r, chunks * share :, :share] = stats_rows(
-                    row_max[mine], row_total[mine], 0.0
+                    row_max[mine], row_total[mine], 0.0, 0.0
                 )
         if n_tp > 1:
             pl.semaphore_wait(barrier, n_tp - 1)
@@ -271,7 +293,7 @@
         def columns(block):
             wide = jnp.concatenate([block[:, :share], jnp.zeros((8, 128 - share))], axis=1)
             turned = wide.T
-            return turned[:share, 0:1], turned[:share, 1:2], turned[:share, 2:3]
+            return [turned[:share, i : i + 1] for i in range(4)]
 
         def joined(block, scale, sums):
             return [
@@ -293,25 +315,38 @@
                 res_sum[r, c * share : (c + 1) * share] = sums[c]
             resident.append((joint, total))
         for p in range(n_seq * n_tp):
-            piece_copy(0, 0, p).wait_recv()
-        pieces = [columns(piece_in[p, tail]) for p in range(n_seq * n_tp)]
+            stat_copy(0, 0, p).wait_recv()
+        pieces = [columns(stat_in[p]) for p in range(n_seq * n_tp)]
         for r in range(rows):
             row_max, row_total = resident[r]
             maxima = [
-                jnp.where(slot == float(r), piece_max, MASKED) for piece_max, _, slot in pieces
+                jnp.where(slot == float(r), piece_max, MASKED) for piece_max, _, slot, _ in pieces
             ]
             joint = functools.reduce(jnp.maximum, maxima, row_max)
-            scale = jnp.exp(row_max - joint)
-            total = row_total * scale
-            sums = [res_sum[r, c * share : (c + 1) * share] * scale for c in range(chunks)]
+            factor = jnp.exp(row_max - joint)
+            factors = [
+                jnp.where(pieces[p][2] == float(r), jnp.exp(maxima[p] - joint), 0.0)
+                for p in range(n_seq * n_tp)
+            ]
+            total = row_total * factor
             for p in range(n_seq * n_tp):
-                scale = jnp.where(
-                    pieces[p][2] == float(r), jnp.exp(maxima[p] - joint), 0.0
-                )
-                total += pieces[p][1] * scale
-                sums = joined(piece_in[p], scale, sums)
+                total += pieces[p][1] * factors[p]
+            inverse = 1.0 / total
+            for p in range(n_seq * n_tp):
+                scales[r, p] = jnp.broadcast_to(factors[p] * pieces[p][3] * inverse, (share, 128))
             for c in range(chunks):
-                out_ref[0, r, :, c * 128 : (c + 1) * 128] = (sums[c] / total).astype(jnp.bfloat16)
+                block = slice(c * share, (c + 1) * share)
+                res_sum[r, block] = res_sum[r, block] * (factor * inverse)
+        for p in range(n_seq * n_tp):
+            piece_copy(0, 0, p).wait_recv()
+        for c in range(chunks):
+            block = slice(c * share, (c + 1) * share)
+            sums = [res_sum[r, block] for r in range(rows)]
+            for p in range(n_seq * n_tp):
+                value = piece_in[p][block].astype(jnp.int32).astype(jnp.float32)
+                sums = [sums[r] + value * scales[r, p] for r in range(rows)]
+            for r in range(rows):
+                out_ref[0, r, :, c * 128 : (c + 1) * 128] = sums[r].astype(out_ref.dtype)
         for k in range(1, n_tp):
             res_copy(lax.rem(tp + k, n_tp), tp).wait_send()
 
@@ -329,7 +364,7 @@
     parts = n_seq * n_tp
     return pl.pallas_call(
         functools.partial(kernel, n_seq, n_tp),
-        out_shape=jax.ShapeDtypeStruct((1, rows, share, latent), jnp.bfloat16),
+        out_shape=jax.ShapeDtypeStruct((1, rows, share, latent), jnp.float32),
         in_specs=[pl.BlockSpec(memory_space=pl.ANY)] * 9,
         out_specs=vmem,
         scratch_shapes=[
@@ -348,8 +383,11 @@
             pltpu.VMEM((n_seq, heads, width), jnp.bfloat16),
             pltpu.VMEM((n_seq, 8, 128), jnp.int32),
             pltpu.VMEM((n_seq, 8, 128), jnp.int32),
-            pltpu.VMEM((n_seq, n_tp, packed, 128), jnp.float32),
-            pltpu.VMEM((parts, packed, 128), jnp.float32),
+            pltpu.VMEM((n_seq, n_tp, packed - 8, 128), jnp.int16),
+            pltpu.VMEM((parts, packed - 8, 128), jnp.int16),
+            pltpu.VMEM((n_seq, n_tp, 8, 128), jnp.float32),
+            pltpu.VMEM((parts, 8, 128), jnp.float32),
+            pltpu.VMEM((rows, parts, share, 128), jnp.float32),
             pltpu.VMEM((n_tp, rows, packed, 128), jnp.float32),
             pltpu.VMEM((n_tp, rows, packed, 128), jnp.float32),
             pltpu.VMEM((rows, packed, 128), jnp.float32),
@@ -358,6 +396,8 @@
             pltpu.SemaphoreType.DMA((n_seq,)),
             pltpu.SemaphoreType.DMA((n_seq,)),
             pltpu.SemaphoreType.DMA((n_seq,)),
+            pltpu.SemaphoreType.DMA((parts,)),
+            pltpu.SemaphoreType.DMA((parts,)),
             pltpu.SemaphoreType.DMA((parts,)),
             pltpu.SemaphoreType.DMA((parts,)),
             pltpu.SemaphoreType.DMA((n_tp,)),
@@ -369,7 +409,7 @@
     )(
         jnp.swapaxes(page_pool, 1, 2), queries, block_table, res_len.T, piece_len,
         piece_owner, piece_slot, piece_pos, kv_gain[None],
-    )
+    ).astype(jnp.bfloat16)
 
 
 def solution(mesh):

time: 24.6 us -> 23.9 us (0.972); the launches traced: 24.2 us -> 23.8 us
  other arithmetic: 0 us -> 1.62 us
  local copies, waits for them, and re-layouts: 1.57 us -> 0 us
  Pallas kernels: 22.6 us -> 22.2 us
    convert_element_type x0 -> x1, other arithmetic: none -> 1.62 us  [local(): return pl.pallas_call(functools.partial(kernel, n_seq, n_tp), out_shape=j...]
    unnamed x1 -> x0, local copies, waits for them, and re-layouts: 1.57 us -> none
    pallas_call x1, Pallas kernels: 22.6 us -> 22.2 us  [local(): pl.pallas_call(functools.partial(kernel, n_seq, n_tp), out_shape=jax.Shap...]
where the time goes in v3:
time: 23.9 us; the launch traced here: 23.8 us
  Pallas kernels  22.2 us (93%)
  other arithmetic  1.62 us (7%)
    pallas_call x1, Pallas kernels, local(): pl.pallas_call(functools.partial(kernel, n_seq, n_tp), out_shape=jax.Shap...  22.2 us
    convert_element_type x1, other arithmetic, local(): return pl.pallas_call(functools.partial(kernel, n_seq, n_tp), out_shape=j...  1.62 us

profile of v3, /device:TPU:1, one launch (start us, length us, event | category | flops | bytes accessed | tf_op | source)
XLA Modules:
  0.0 23.8 jit_solution(3893881812533469254)
XLA Ops:
  0.0 22.2 %shard_map.91 = f32[1,4,32,512]{3,2,1,0:T(8,128)} custom-call(bf16[12,576,128]{2,1,0:T(8,128)(2,1)} %bitcast.3, bf16[4,64,576]{2,1,0:T(8,128)(2,1)} %q_hbm.1, s32[4,1,4]{2,1,0:T(1,128)} %table_hbm.1, s32[1,4]{1,0:T(1,128)} %bitcast.5, s32[1,1,4]{2,1,0:T(1,128)} %len_hbm.1, s32[1,1,4]{2,1,0:T(1,128)} %owner_hbm.1, s32[1,1,4]{2,1,0:T(1,128)} %slot_hbm.1, ...), custom_call_target="tpu_custom_call" | custom-call | tf_op jit(solution)/shard_map/pallas_call | solution.py:365
  22.2 1.6 %convert_element_type.3 = bf16[1,4,32,512]{3,2,1,0:T(8,128)(2,1)} convert(f32[1,4,32,512]{3,2,1,0:T(8,128)} %shard_map.91) | non-fusion elementwise | flops 65536 | bytes 393216 | tf_op jit(solution)/shard_map/convert_element_type | solution.py:412

commit v4 on v3

--- a/solution.py
+++ b/solution.py
@@ -68,8 +68,8 @@
     tp = lax.axis_index("tp")
     section = lax.axis_index("section")
     barrier = pltpu.get_barrier_semaphore()
-    order = [lax.rem((seq // 2) * 2 + 2 + i, n_seq) for i in range(n_seq)]
-    peers = order[: n_seq - 2] + [(seq // 2) * 2 + 1 - lax.rem(seq, 2)]
+    order = [lax.rem((seq // 2) * 2 + i, n_seq) for i in range(n_seq)]
+    peers = [(seq // 2) * 2 + 1 - lax.rem(seq, 2)] + order[2:]
 
     loads = [
         pltpu.make_async_copy(source, target, load_sem.at[i])
@@ -81,9 +81,6 @@
             ]
         )
     ]
-    for load in loads:
-        load.start()
-
     def at(s, t, c):
         return {"seq": s, "tp": t, "section": c}
 
@@ -122,9 +119,11 @@
         raw_copy = pltpu.make_async_copy(
             pool_hbm.at[pl.ds(0, fresh_pages)], pool.at[pl.ds(0, fresh_pages)], pool_sem
         )
-        raw_copy.start()
         for peer in peers:
             pl.semaphore_signal(barrier, inc=1, device_id=at(peer, tp, 0), device_id_type=MESH)
+        for load in loads:
+            load.start()
+        raw_copy.start()
         for load in loads:
             load.wait()
 
@@ -191,7 +190,7 @@
         out_ref[...] = jnp.zeros_like(out_ref)
         tokens = lax.broadcasted_iota(jnp.int32, (1, FRESH_DEV), 1)
         for first in range(0, n_seq, GROUP):
-            for d in peers[first : first + GROUP]:
+            for d in peers[max(first - 1, 0) : first + GROUP - 1]:
                 q_copy(d, d).wait_recv()
             members = range(first, first + GROUP)
             wide = jnp.concatenate([q_in[order[i]] for i in members], axis=0)
@@ -247,7 +246,6 @@
     @pl.when(section == 1)
     def decode():
         pool_copy = pltpu.make_async_copy(pool_hbm, pool, pool_sem)
-        pool_copy.start()
         for s in range(n_seq):
             for t in range(n_tp):
                 pl.semaphore_signal(barrier, inc=1, device_id=at(s, t, 0), device_id_type=MESH)
@@ -255,6 +253,9 @@
             pl.semaphore_signal(
                 barrier, inc=1, device_id=at(seq, lax.rem(tp + k, n_tp), 1), device_id_type=MESH
             )
+        for load in loads:
+            load.start()
+        pool_copy.start()
         for load in loads:
             load.wait()
         pool_copy.wait()
@@ -364,8 +365,8 @@
     parts = n_seq * n_tp
     return pl.pallas_call(
         functools.partial(kernel, n_seq, n_tp),
-        out_shape=jax.ShapeDtypeStruct((1, rows, share, latent), jnp.float32),
-        in_specs=[pl.BlockSpec(memory_space=pl.ANY)] * 9,
+        out_shape=jax.ShapeDtypeStruct((1, rows, share, latent), jnp.bfloat16),
+        in_specs=[pl.BlockSpec(memory_space=pltpu.HBM)] * 9,
         out_specs=vmem,
         scratch_shapes=[
             pltpu.VMEM(queries.shape, jnp.bfloat16),
@@ -404,12 +405,17 @@
             pltpu.SemaphoreType.DMA((n_tp,)),
         ],
         compiler_params=pltpu.CompilerParams(
-            collective_id=0, has_side_effects=True, vmem_limit_bytes=56 * 1024 * 1024
+            collective_id=0, has_side_effects=True, vmem_limit_bytes=32 * 1024 * 1024
         ),
     )(
-        jnp.swapaxes(page_pool, 1, 2), queries, block_table, res_len.T, piece_len,
-        piece_owner, piece_slot, piece_pos, kv_gain[None],
-    ).astype(jnp.bfloat16)
+        *[
+            pltpu.with_memory_space_constraint(operand, pltpu.HBM)
+            for operand in (
+                jnp.swapaxes(page_pool, 1, 2), queries, block_table, res_len.T, piece_len,
+                piece_owner, piece_slot, piece_pos, kv_gain[None],
+            )
+        ]
+    )
 
 
 def solution(mesh):

time: 23.9 us -> 22.3 us (0.933)
  other arithmetic: 1.62 us -> 0 us
  Pallas kernels: 22.2 us -> 21.4 us
  local copies, waits for them, and re-layouts: 0 us -> 0.66 us
    convert_element_type x1 -> x0, other arithmetic: 1.62 us -> none  [local(): return pl.pallas_call(functools.partial(kernel, n_seq, n_tp), out_shape=j...]
    pallas_call x1, Pallas kernels: 22.2 us -> 21.4 us  [local(): pl.pallas_call(functools.partial(kernel, n_seq, n_tp), out_shape=jax.Shap...]
    unnamed x0 -> x1, local copies, waits for them, and re-layouts: none -> 0.66 us
where the time goes in v4:
time: 22.3 us; the launch traced here: 22.1 us
  Pallas kernels  21.4 us (96%)
  local copies, waits for them, and re-layouts  0.66 us (3%)
    pallas_call x1, Pallas kernels, local(): pl.pallas_call(functools.partial(kernel, n_seq, n_tp), out_shape=jax.Shap...  21.4 us
    unnamed x1, local copies, waits for them, and re-layouts  0.66 us

profile of v4, /device:TPU:1, one launch (start us, length us, event | category | flops | bytes accessed | tf_op | source)
XLA Modules:
  0.0 22.1 jit_solution(14106654873554761264)
XLA Ops:
  0.0 21.4 %shard_map.91 = bf16[1,4,32,512]{3,2,1,0:T(8,128)(2,1)S(1)} custom-call(bf16[12,576,128]{2,1,0:T(8,128)(2,1)} %bitcast.3, bf16[4,64,576]{2,1,0:T(8,128)(2,1)} %q_hbm.1, s32[4,1,4]{2,1,0:T(1,128)} %table_hbm.1, s32[1,4]{1,0:T(1,128)} %bitcast.5, s32[1,1,4]{2,1,0:T(1,128)} %len_hbm.1, s32[1,1,4]{2,1,0:T(1,128)} %owner_hbm.1, s32[1,1,4]{2,1,0:T(1,128)} %slot_hbm.1, ...), custom_call_target="tpu_custom_call" | custom-call | tf_op jit(solution)/shard_map/pallas_call | solution.py:366
  21.4 0.7 %copy.11 = bf16[1,4,32,512]{3,2,1,0:T(8,128)(2,1)} copy(bf16[1,4,32,512]{3,2,1,0:T(8,128)(2,1)S(1)} %shard_map.91) | data formatting | bytes 262144

commit v5 on v4

--- a/solution.py
+++ b/solution.py
@@ -211,15 +211,19 @@
                 (((1,), (1,)), ((), ())), preferred_element_type=jnp.float32,
             )
             step = jnp.maximum(jnp.max(jnp.abs(group_out), axis=1, keepdims=True), 1e-30) / STEPS
+            turned = stats_rows(
+                jnp.concatenate([stats[i - first][0] for i in members], axis=0),
+                jnp.concatenate([stats[i - first][1] for i in members], axis=0),
+                jnp.concatenate(
+                    [jnp.full((heads, 1), stats[i - first][2], jnp.float32) for i in members],
+                    axis=0,
+                ),
+                step,
+            )
             for i in members:
-                row_max, row_total, slot = stats[i - first]
-                here = (i - first) * heads
                 for t in range(n_tp):
-                    mine = slice(t * share, (t + 1) * share)
-                    stat_out[i, t, :, :share] = stats_rows(
-                        row_max[mine], row_total[mine], slot,
-                        step[here + t * share : here + (t + 1) * share],
-                    )
+                    here = (i - first) * heads + t * share
+                    stat_out[i, t, :, :share] = turned[:, here : here + share]
                     stat_copy(i, t, seq * n_tp + tp).start()
             counted = jnp.floor(group_out * (1.0 / step) + 0.5)
             for i in members:
@@ -314,30 +318,38 @@
                 sums = joined(res_in[t, r], scale, sums)
             for c in range(chunks):
                 res_sum[r, c * share : (c + 1) * share] = sums[c]
+            lines = [res_in[t, r, tail] for t in range(n_tp)]
+            joint = functools.reduce(jnp.maximum, [line[0:1] for line in lines])
+            total = sum(line[1:2] * jnp.exp(line[0:1] - joint) for line in lines)
             resident.append((joint, total))
         for p in range(n_seq * n_tp):
             stat_copy(0, 0, p).wait_recv()
-        pieces = [columns(stat_in[p]) for p in range(n_seq * n_tp)]
+        count = n_seq * n_tp
+        piece_max, piece_total, piece_slot, piece_step = [stat_in[:, i, :] for i in range(4)]
+        mixed, kept = [], []
         for r in range(rows):
             row_max, row_total = resident[r]
-            maxima = [
-                jnp.where(slot == float(r), piece_max, MASKED) for piece_max, _, slot, _ in pieces
-            ]
-            joint = functools.reduce(jnp.maximum, maxima, row_max)
+            member = piece_slot == float(r)
+            maxima = jnp.where(member, piece_max, MASKED)
+            joint = jnp.maximum(jnp.max(maxima, axis=0, keepdims=True), row_max)
             factor = jnp.exp(row_max - joint)
-            factors = [
-                jnp.where(pieces[p][2] == float(r), jnp.exp(maxima[p] - joint), 0.0)
-                for p in range(n_seq * n_tp)
-            ]
-            total = row_total * factor
-            for p in range(n_seq * n_tp):
-                total += pieces[p][1] * factors[p]
+            factors = jnp.where(member, jnp.exp(maxima - joint), 0.0)
+            total = row_total * factor + jnp.sum(piece_total * factors, axis=0, keepdims=True)
             inverse = 1.0 / total
-            for p in range(n_seq * n_tp):
-                scales[r, p] = jnp.broadcast_to(factors[p] * pieces[p][3] * inverse, (share, 128))
+            mixed.append(factors * piece_step * inverse)
+            kept.append(factor * inverse)
+        used = rows * count + rows
+        mixed += kept + [jnp.zeros((-used % 128, 128), jnp.float32)]
+        turned = jnp.concatenate(mixed, axis=0).T
+        for r in range(rows):
+            for p in range(count):
+                at_p = r * count + p
+                scales[r, p] = jnp.broadcast_to(turned[:share, at_p : at_p + 1], (share, 128))
+            at_r = rows * count + r
+            factor = turned[:share, at_r : at_r + 1]
             for c in range(chunks):
                 block = slice(c * share, (c + 1) * share)
-                res_sum[r, block] = res_sum[r, block] * (factor * inverse)
+                res_sum[r, block] = res_sum[r, block] * factor
         for p in range(n_seq * n_tp):
             piece_copy(0, 0, p).wait_recv()
         for c in range(chunks):

time: 22.3 us -> 21.2 us (0.951)
  Pallas kernels: 21.4 us -> 20.3 us
    pallas_call x1, Pallas kernels: 21.4 us -> 20.3 us  [local(): pl.pallas_call(functools.partial(kernel, n_seq, n_tp), out_shape=jax.Shap...]
where the time goes in v5:
time: 21.2 us; the launch traced here: 21 us
  Pallas kernels  20.3 us (96%)
  local copies, waits for them, and re-layouts  0.66 us (3%)
    pallas_call x1, Pallas kernels, local(): pl.pallas_call(functools.partial(kernel, n_seq, n_tp), out_shape=jax.Shap...  20.3 us
    unnamed x1, local copies, waits for them, and re-layouts  0.66 us

profile of v5, /device:TPU:1, one launch (start us, length us, event | category | flops | bytes accessed | tf_op | source)
XLA Modules:
  0.0 21.0 jit_solution(10400093524292759456)
XLA Ops:
  0.0 20.3 %shard_map.91 = bf16[1,4,32,512]{3,2,1,0:T(8,128)(2,1)S(1)} custom-call(bf16[12,576,128]{2,1,0:T(8,128)(2,1)} %bitcast.3, bf16[4,64,576]{2,1,0:T(8,128)(2,1)} %q_hbm.1, s32[4,1,4]{2,1,0:T(1,128)} %table_hbm.1, s32[1,4]{1,0:T(1,128)} %bitcast.5, s32[1,1,4]{2,1,0:T(1,128)} %len_hbm.1, s32[1,1,4]{2,1,0:T(1,128)} %owner_hbm.1, s32[1,1,4]{2,1,0:T(1,128)} %slot_hbm.1, ...), custom_call_target="tpu_custom_call" | custom-call | tf_op jit(solution)/shard_map/pallas_call | solution.py:378
  20.3 0.7 %copy.11 = bf16[1,4,32,512]{3,2,1,0:T(8,128)(2,1)} copy(bf16[1,4,32,512]{3,2,1,0:T(8,128)(2,1)S(1)} %shard_map.91) | data formatting | bytes 262144

commit v6 on v5

--- a/solution.py
+++ b/solution.py
@@ -350,16 +350,22 @@
             for c in range(chunks):
                 block = slice(c * share, (c + 1) * share)
                 res_sum[r, block] = res_sum[r, block] * factor
-        for p in range(n_seq * n_tp):
-            piece_copy(0, 0, p).wait_recv()
-        for c in range(chunks):
-            block = slice(c * share, (c + 1) * share)
-            sums = [res_sum[r, block] for r in range(rows)]
-            for p in range(n_seq * n_tp):
-                value = piece_in[p][block].astype(jnp.int32).astype(jnp.float32)
-                sums = [sums[r] + value * scales[r, p] for r in range(rows)]
-            for r in range(rows):
-                out_ref[0, r, :, c * 128 : (c + 1) * 128] = sums[r].astype(out_ref.dtype)
+        near = [order[i] * n_tp + t for i in range(2) for t in range(n_tp)]
+        far = [order[i] * n_tp + t for i in range(2, n_seq) for t in range(n_tp)]
+        for last, arriving in ((False, near), (True, far)):
+            for p in arriving:
+                piece_copy(0, 0, p).wait_recv()
+            for c in range(chunks):
+                block = slice(c * share, (c + 1) * share)
+                sums = [res_sum[r, block] for r in range(rows)]
+                for p in arriving:
+                    value = piece_in[p, block].astype(jnp.int32).astype(jnp.float32)
+                    sums = [sums[r] + value * scales[r, p] for r in range(rows)]
+                for r in range(rows):
+                    if last:
+                        out_ref[0, r, :, c * 128 : (c + 1) * 128] = sums[r].astype(out_ref.dtype)
+                    else:
+                        res_sum[r, block] = sums[r]
         for k in range(1, n_tp):
             res_copy(lax.rem(tp + k, n_tp), tp).wait_send()
 

time: 21.2 us -> 21.1 us (level)
  no operation moved by 1% of the time
where the time goes in v6:
time: 21.1 us; the launch traced here: 21 us
  Pallas kernels  20.3 us (96%)
  local copies, waits for them, and re-layouts  0.66 us (3%)
    pallas_call x1, Pallas kernels, local(): pl.pallas_call(functools.partial(kernel, n_seq, n_tp), out_shape=jax.Shap...  20.3 us
    unnamed x1, local copies, waits for them, and re-layouts  0.66 us

profile of v6, /device:TPU:1, one launch (start us, length us, event | category | flops | bytes accessed | tf_op | source)
XLA Modules:
  0.0 21.0 jit_solution(551117262147836291)
XLA Ops:
  0.0 20.3 %shard_map.91 = bf16[1,4,32,512]{3,2,1,0:T(8,128)(2,1)S(1)} custom-call(bf16[12,576,128]{2,1,0:T(8,128)(2,1)} %bitcast.3, bf16[4,64,576]{2,1,0:T(8,128)(2,1)} %q_hbm.1, s32[4,1,4]{2,1,0:T(1,128)} %table_hbm.1, s32[1,4]{1,0:T(1,128)} %bitcast.5, s32[1,1,4]{2,1,0:T(1,128)} %len_hbm.1, s32[1,1,4]{2,1,0:T(1,128)} %owner_hbm.1, s32[1,1,4]{2,1,0:T(1,128)} %slot_hbm.1, ...), custom_call_target="tpu_custom_call" | custom-call | tf_op jit(solution)/shard_map/pallas_call | solution.py:384
  20.3 0.7 %copy.11 = bf16[1,4,32,512]{3,2,1,0:T(8,128)(2,1)} copy(bf16[1,4,32,512]{3,2,1,0:T(8,128)(2,1)S(1)} %shard_map.91) | data formatting | bytes 262144

commit v7 on v5

--- a/solution.py
+++ b/solution.py
@@ -146,10 +146,10 @@
             meta_out[d] = jnp.full(meta_out.shape[1:], owner_slot[i], jnp.int32)
 
         pl.semaphore_wait(barrier, n_seq - 1 + n_seq * n_tp)
-        for peer in peers:
+        for peer in peers[1:] + peers[:1]:
             meta_copy(peer, seq).start()
 
-        for peer in peers:
+        for peer in peers[1:] + peers[:1]:
             meta_copy(peer, peer).wait_recv()
             wanted = meta_in[peer][0:1, 0:1]
             picked = q_ref[0].astype(jnp.float32)

time: 21.2 us -> 21.8 us (1.028)
  Pallas kernels: 20.3 us -> 21 us
    pallas_call x1, Pallas kernels: 20.3 us -> 21 us  [local(): pl.pallas_call(functools.partial(kernel, n_seq, n_tp), out_shape=jax.Shap...]
where the time goes in v7:
time: 21.8 us; the launch traced here: 21.7 us
  Pallas kernels  21 us (96%)
  local copies, waits for them, and re-layouts  0.66 us (3%)
    pallas_call x1, Pallas kernels, local(): pl.pallas_call(functools.partial(kernel, n_seq, n_tp), out_shape=jax.Shap...  21 us
    unnamed x1, local copies, waits for them, and re-layouts  0.66 us

profile of v7, /device:TPU:1, one launch (start us, length us, event | category | flops | bytes accessed | tf_op | source)
XLA Modules:
  0.0 21.7 jit_solution(6838629669494812521)
XLA Ops:
  0.0 21.0 %shard_map.91 = bf16[1,4,32,512]{3,2,1,0:T(8,128)(2,1)S(1)} custom-call(bf16[12,576,128]{2,1,0:T(8,128)(2,1)} %bitcast.3, bf16[4,64,576]{2,1,0:T(8,128)(2,1)} %q_hbm.1, s32[4,1,4]{2,1,0:T(1,128)} %table_hbm.1, s32[1,4]{1,0:T(1,128)} %bitcast.5, s32[1,1,4]{2,1,0:T(1,128)} %len_hbm.1, s32[1,1,4]{2,1,0:T(1,128)} %owner_hbm.1, s32[1,1,4]{2,1,0:T(1,128)} %slot_hbm.1, ...), custom_call_target="tpu_custom_call" | custom-call | tf_op jit(solution)/shard_map/pallas_call | solution.py:378
  21.0 0.7 %copy.11 = bf16[1,4,32,512]{3,2,1,0:T(8,128)(2,1)} copy(bf16[1,4,32,512]{3,2,1,0:T(8,128)(2,1)S(1)} %shard_map.91) | data formatting | bytes 262144
